TPU v7x, 32 devices: a whole 2x2x4 slice. The times are simulated.
32 devices in a mesh: clus: 4 (over y, x), leaf: 8 (over z, core).
Axes of the slice: x: 2, y: 2, z: 4, core: 2. Of those that a mesh axis runs over, the one named last changes fastest.
Arguments:
- points: bfloat16 [64, 65536], P(None, ('clus', 'leaf')), may hold values from -6 to 6
- weights: bfloat16 [512, 65536], P(None, ('clus', 'leaf')), may hold values from -2 to 2
- targets: bfloat16 [512, 65536], P(None, ('clus', 'leaf')), may hold values from -6 to 6
- near_lists: int32 [128, 4], P(('clus', 'leaf')), may hold values from 0 to 127, as said below
- tile_counts: int32 [128], P(('clus', 'leaf')), may hold values from 2 to 4, as said below
- skeleton: int32 [32, 256], P(('clus', 'leaf')), may hold values from 0 to 2047, as said below
Outputs:
- precond: float32 [512, 65536], P(None, ('clus', 'leaf'))
Inputs may be any that keep to these rules, and one draw needn't show every extreme that they name: `near_lists`: row g lists cluster ids; its first entry is g; its first tile_counts[g] entries are distinct, and the rest repeat g. Every listed cluster lies on a device with the same leaf index as cluster g's device and a clus index at most 1 away; some cluster lists one exactly 1 away. `tile_counts`: some cluster has exactly 4 tiles. `skeleton`: each row holds 256 distinct indices of points of its device; their order matters.
All inputs are finite; a program needn't handle non-finite values.
Results may differ from a plain program's by a relative error of at most 0.0039.
Values may be sent and summed in bfloat16 or wider, within the bound.
A program may use at most 128 MiB of HBM per device.

v0:
```python
import functools

import jax
import jax.numpy as jnp
from jax import lax
from jax.experimental import pallas as pl
from jax.experimental.pallas import tpu as pltpu
from jax.sharding import PartitionSpec as P

ridge_term = 0.5
node_shift = 4.0
MESH = pl.DeviceIdType.MESH
F32 = jnp.float32
BF16 = jnp.bfloat16
SWEEP = 8
LOG2E = 1.4426950408889634
PIECE = 64
CHUNK = 128


def dot(a, b):
    return jnp.dot(a, b, preferred_element_type=F32)


def dot_full(a, b, dims=((1,), (0,))):
    return lax.dot_general(
        a, b, (dims, ((), ())), precision=lax.Precision.HIGHEST, preferred_element_type=F32
    )


def split(a):
    high = a.astype(BF16)
    return high, (a - high.astype(F32)).astype(BF16)


def dot_split(a, b_high, b_low):
    a_high, a_low = split(a)
    return dot(a_high, b_high) + dot(a_low, b_high) + dot(a_high, b_low)


def square_cols(pts):
    wide = pts.astype(F32)
    return dot_full(wide * wide, jnp.ones((pts.shape[0], 128), F32), ((0,), (0,)))


def square_rows(pts):
    wide = pts.astype(F32)
    return jnp.sum(wide * wide, axis=0, keepdims=True)


def kernel_tile(row_pts, row_sq, col_pts, col_sq, bias=0.0):
    scale = 2.0 / row_pts.shape[0] * LOG2E
    cross = lax.dot_general(
        row_pts, col_pts, (((0,), (0,)), ((), ())), preferred_element_type=F32
    )
    row_wide = jnp.concatenate([row_sq * -scale] * (col_pts.shape[1] // 128), axis=1)
    return jnp.exp2(cross * (2.0 * scale) + (row_wide + (col_sq * -scale + bias)))


def sweep_inverse(mats):
    count, size = mats.shape[0], mats.shape[1]
    row_id = lax.broadcasted_iota(jnp.int32, (count, size, 1), 1)
    col_id = lax.broadcasted_iota(jnp.int32, (count, 1, size), 2)

    def group(_, a):
        for i in range(SWEEP):
            row = a[:, i : i + 1, :]
            col = a[:, :, i : i + 1]
            inv = 1.0 / a[:, i : i + 1, i : i + 1]
            row = jnp.where(col_id == i, -inv, row * inv)
            col = jnp.where(row_id == i, -1.0, col)
            rest = jnp.where((row_id == i) | (col_id == i), 0.0, a)
            a = rest - col * row
        a = jnp.concatenate([a[:, SWEEP:, :], a[:, :SWEEP, :]], axis=1)
        return pltpu.roll(a, size - SWEEP, 2)

    return -lax.fori_loop(0, size // SWEEP, group, mats)


def fused_kernel(
    n_clus, n_leaf,
    points, weights, targets, bias, skeleton,
    out,
    window, win_p, win_sq, tiles, pick, prolong, gram, inv_high, inv_low, node_p, got_p,
    node_r, got_r, sent_r, solved_buf,
    ps, pr, as_, ar, bs, br, qs, qr, ts, tr,
):
    clus, leaf = lax.axis_index("clus"), lax.axis_index("leaf")
    levels = n_leaf.bit_length() - 1
    clusters = bias.shape[0] // 3
    pts_cl = points.shape[1] // clusters
    n_skel = skeleton.shape[1]
    half = n_skel // 2
    n_piece = weights.shape[0] // PIECE
    n_ch = weights.shape[0] // CHUNK
    even = lax.rem(clus, 2) == 0
    partner = jnp.where(even, clus + 1, clus - 1)
    onward = jnp.where(even, clus + 2, clus - 2)
    behind = jnp.where(even, clus - 2, clus + 2)
    has_onward = (onward >= 0) & (onward < n_clus)
    has_behind = (behind >= 0) & (behind < n_clus)
    siblings = []
    for level in range(levels):
        upper = lax.rem(leaf // (1 << level), 2) == 1
        siblings.append((upper, jnp.where(upper, leaf - (1 << level), leaf + (1 << level))))

    barrier = pltpu.get_barrier_semaphore()
    pl.semaphore_signal(barrier, inc=1, device_id=(partner, leaf), device_id_type=MESH)
    for _, sibling in siblings:
        pl.semaphore_signal(barrier, inc=1, device_id=(clus, sibling), device_id_type=MESH)

    @pl.when(has_onward)
    def _():
        pl.semaphore_signal(barrier, inc=1, device_id=(onward, leaf), device_id_type=MESH)

    @pl.when(has_behind)
    def _():
        pl.semaphore_signal(barrier, inc=1, device_id=(behind, leaf), device_id_type=MESH)

    pl.semaphore_wait(
        barrier, 1 + levels + has_onward.astype(jnp.int32) + has_behind.astype(jnp.int32)
    )

    def remote(src, dst, send, recv, where):
        return pltpu.make_async_remote_copy(
            src_ref=src, dst_ref=dst, send_sem=send, recv_sem=recv, device_id=where,
            device_id_type=MESH,
        )

    first_p = remote(points, win_p.at[1], ps.at[0], pr.at[0], (partner, leaf))
    next_p = remote(win_p.at[1], win_p.at[2], ps.at[1], pr.at[1], (onward, leaf))
    first_p.start()
    first_w, next_w = [], []
    for i in range(n_piece):
        rows = pl.ds(i * PIECE, PIECE)
        first_w.append(remote(
            weights.at[rows], window.at[0, rows], as_.at[i], ar.at[i], (partner, leaf)
        ))
        next_w.append(remote(
            window.at[0, rows], window.at[1, rows], bs.at[i], br.at[i], (onward, leaf)
        ))
        first_w[i].start()

    def pass_on(first, after):
        first.wait_recv()

        @pl.when(has_onward)
        def _():
            after.start()

    @pl.when(jnp.logical_not(has_behind))
    def _():
        win_p[2] = jnp.zeros(points.shape, BF16)
        window[1] = jnp.zeros(weights.shape, BF16)

    def take(after):
        @pl.when(has_behind)
        def _():
            after.wait_recv()

    skel = skeleton[...]
    pick[...] = (
        lax.broadcasted_iota(jnp.int32, (points.shape[1], n_skel), 0) == skel
    ).astype(BF16)
    base_p = dot(points[...], pick[...]).astype(BF16)
    node_p[0] = base_p
    for level, (upper, sibling) in enumerate(siblings):
        copy = remote(
            node_p.at[level, :, pl.ds(0, half)], got_p.at[level], qs.at[level], qr.at[level],
            (clus, sibling),
        )
        copy.start()
        copy.wait()
        mine, other = node_p[level, :, :half], got_p[level]
        node_p[level + 1, :, :half] = jnp.where(upper, other, mine)
        node_p[level + 1, :, half:] = jnp.where(upper, mine, other)

    pass_on(first_p, next_p)
    win_p[0] = points[...]
    for level in range(levels + 1):
        p = node_p[level]
        shift_mat = jnp.where(
            lax.broadcasted_iota(jnp.int32, (n_skel, n_skel), 0)
            == lax.broadcasted_iota(jnp.int32, (n_skel, n_skel), 1),
            node_shift, 0.0,
        )
        gram[level] = kernel_tile(p, square_cols(p), p, square_rows(p)) + shift_mat

    own_sq_cols = square_cols(base_p)
    own_sq = square_rows(points[...])
    for k in range(clusters):
        cols = slice(k * pts_cl, (k + 1) * pts_cl)
        prolong[:, cols] = kernel_tile(
            base_p, own_sq_cols, points[:, cols], own_sq[:, cols]
        ).astype(BF16)

    top_inv = sweep_inverse(gram[:, :half, :half])
    couple = [dot_full(top_inv[v], gram[v, :half, half:]) for v in range(levels + 1)]
    schur = jnp.stack([
        gram[v, half:, half:] - dot_full(gram[v, half:, :half], couple[v])
        for v in range(levels + 1)
    ])
    pass_on(first_w[0], next_w[0])
    pass_on(first_w[1], next_w[1])
    low_inv = sweep_inverse(schur)
    pass_on(first_w[2], next_w[2])
    pass_on(first_w[3], next_w[3])
    for v in range(levels + 1):
        cross = dot_full(couple[v], low_inv[v])
        corner = top_inv[v] + dot_full(cross, couple[v], ((1,), (1,)))
        whole = jnp.concatenate([
            jnp.concatenate([corner, -cross], axis=1),
            jnp.concatenate([-cross.T, low_inv[v]], axis=1),
        ], axis=0)
        inv_high[v], inv_low[v] = split(whole)

    take(next_p)
    for place in range(3):
        win_sq[...] = square_cols(win_p[place])

        def build(r, _):
            rows = pl.ds(pl.multiple_of(r * 128, 128), 128)
            q = pl.ds(place * clusters + r * 128 // pts_cl, 1)
            for k in range(clusters):
                cols = slice(k * pts_cl, (k + 1) * pts_cl)
                tiles[place, rows, cols] = kernel_tile(
                    win_p[place, :, rows], win_sq[rows, :],
                    points[:, cols], own_sq[:, cols], bias[q, cols],
                ).astype(BF16)
            return 0

        lax.fori_loop(0, points.shape[1] // 128, build, 0)

    per = CHUNK // PIECE
    passed = 4

    def exchange(c, level):
        at = c * levels + level
        return remote(
            sent_r.at[at], got_r.at[at], ts.at[at], tr.at[at], (clus, siblings[level][1])
        )

    def climb(c, level, node_res):
        solved = dot_split(node_res, inv_high[level], inv_low[level])
        solved_buf[c * levels + level] = solved
        sent_r[c * levels + level] = node_shift * solved[:, :half]
        exchange(c, level).start()

    def joined(c, level):
        exchange(c, level).wait()
        mine, other = sent_r[c * levels + level], got_r[c * levels + level]
        upper = siblings[level][0]
        return jnp.concatenate(
            [jnp.where(upper, other, mine), jnp.where(upper, mine, other)], axis=1
        )

    def near_stage(c):
        span = slice(c * CHUNK, (c + 1) * CHUNK)
        for i in range(max(passed, c * per), (c + 1) * per):
            pass_on(first_w[i], next_w[i])
        @pl.loop(0, clusters)
        def _(k):
            cols = pl.ds(pl.multiple_of(k * pts_cl, pts_cl), pts_cl)
            near = dot(weights[span, :], tiles[0, :, cols]) + dot(
                window[0, span, :], tiles[1, :, cols]
            )
            out[span, cols] = (
                targets[span, cols].astype(F32) - ridge_term * weights[span, cols].astype(F32)
                - near
            )
        for i in range(c * per, (c + 1) * per):
            take(next_w[i])
        node_r[...] = jnp.zeros_like(node_r)

        @pl.loop(0, clusters)
        def _(k):
            cols = pl.ds(pl.multiple_of(k * pts_cl, pts_cl), pts_cl)
            residual = out[span, cols] - dot(window[1, span, :], tiles[2, :, cols])
            out[span, cols] = residual
            high, low = split(residual)
            node_r[...] += dot(high, pick[cols, :]) + dot(low, pick[cols, :])
        climb(c, 0, node_r[...])

    def last_stage(c):
        span = slice(c * CHUNK, (c + 1) * CHUNK)
        correction = dot_split(joined(c, levels - 1), inv_high[levels], inv_low[levels])
        for level in reversed(range(levels)):
            upper = siblings[level][0]
            inject = jnp.where(upper, correction[:, half:], correction[:, :half])
            correction = solved_buf[c * levels + level] + jnp.concatenate(
                [inject, jnp.zeros_like(inject)], axis=1
            )
        high, low = split(correction)

        @pl.loop(0, clusters)
        def _(k):
            cols = pl.ds(pl.multiple_of(k * pts_cl, pts_cl), pts_cl)
            placed = lax.dot_general(
                jnp.concatenate([high, low], axis=0), pick[cols, :], (((1,), (1,)), ((), ())),
                preferred_element_type=F32,
            )
            out[span, cols] = (
                out[span, cols] * (1.0 / (1.0 + ridge_term)) + dot(high, prolong[:, cols])
                + (placed[:CHUNK] + placed[CHUNK:])
            )

    for step in range(n_ch + levels):
        for stage in reversed(range(levels + 1)):
            c = step - stage
            if not 0 <= c < n_ch:
                continue
            if stage == 0:
                near_stage(c)
            elif stage < levels:
                climb(c, stage, joined(c, stage - 1))
            else:
                last_stage(c)

    first_p.wait_send()
    for i in range(n_piece):
        first_w[i].wait_send()

    @pl.when(has_onward)
    def _():
        next_p.wait_send()
        for i in range(n_piece):
            next_w[i].wait_send()


def near_bias(n_clus, n_leaf, pts_cl, near_lists, tile_counts):
    clus, leaf = lax.axis_index("clus"), lax.axis_index("leaf")
    clusters, slots = near_lists.shape
    even = lax.rem(clus, 2) == 0
    partner = jnp.where(even, clus + 1, clus - 1)
    other = jnp.where(even, clus - 1, clus + 1)
    place = jnp.stack([clus, partner, other])
    valid = (place >= 0) & (place < n_clus)
    first = jnp.where(valid, (place * n_leaf + leaf) * clusters, -clusters)
    ident = (first[:, None] + jnp.arange(clusters)[None, :]).reshape(-1)
    used = jnp.arange(slots)[None, :] < tile_counts[:, None]
    hit = (near_lists[:, :, None] == ident[None, None, :]) & used[:, :, None]
    bias = jnp.where(jnp.any(hit, axis=1), 0.0, -1e30).astype(F32)
    return jnp.repeat(bias.T, pts_cl, axis=1)


def on_device(n_clus, n_leaf, points, weights, targets, near_lists, tile_counts, skeleton):
    rhs, pts = weights.shape
    features = points.shape[0]
    clusters = near_lists.shape[0]
    n_skel = skeleton.shape[1]
    half = n_skel // 2
    levels = n_leaf.bit_length() - 1
    n_piece, n_ch = rhs // PIECE, rhs // CHUNK
    vmem = pl.BlockSpec(memory_space=pltpu.VMEM)
    dma = pltpu.SemaphoreType.DMA
    bias = near_bias(n_clus, n_leaf, pts // clusters, near_lists, tile_counts)
    return pl.pallas_call(
        functools.partial(fused_kernel, n_clus, n_leaf),
        out_shape=jax.ShapeDtypeStruct((rhs, pts), F32),
        in_specs=[vmem] * 5,
        out_specs=vmem,
        scratch_shapes=[
            pltpu.VMEM((2, rhs, pts), BF16),
            pltpu.VMEM((3, features, pts), BF16),
            pltpu.VMEM((pts, 128), F32),
            pltpu.VMEM((3, pts, pts), BF16),
            pltpu.VMEM((pts, n_skel), BF16),
            pltpu.VMEM((n_skel, pts), BF16),
            pltpu.VMEM((levels + 1, n_skel, n_skel), F32),
            pltpu.VMEM((levels + 1, n_skel, n_skel), BF16),
            pltpu.VMEM((levels + 1, n_skel, n_skel), BF16),
            pltpu.VMEM((levels + 1, features, n_skel), BF16),
            pltpu.VMEM((levels, features, half), BF16),
            pltpu.VMEM((CHUNK, n_skel), F32),
            pltpu.VMEM((n_ch * levels, CHUNK, half), F32),
            pltpu.VMEM((n_ch * levels, CHUNK, half), F32),
            pltpu.VMEM((n_ch * levels, CHUNK, n_skel), F32),
            dma((2,)), dma((2,)),
            dma((n_piece,)), dma((n_piece,)), dma((n_piece,)), dma((n_piece,)),
            dma((levels,)), dma((levels,)),
            dma((n_ch * levels,)), dma((n_ch * levels,)),
        ],
        compiler_params=pltpu.CompilerParams(
            collective_id=0, has_side_effects=True, vmem_limit_bytes=60 * 1024 * 1024
        ),
    )(points, weights, targets, bias, skeleton)


def solution(mesh):
    placed = (
        P(None, ("clus", "leaf")),
        P(None, ("clus", "leaf")),
        P(None, ("clus", "leaf")),
        P(("clus", "leaf"), None),
        P(("clus", "leaf")),
        P(("clus", "leaf"), None),
    )
    return jax.shard_map(
        functools.partial(on_device, mesh.shape["clus"], mesh.shape["leaf"]),
        mesh=mesh, in_specs=placed, out_specs=P(None, ("clus", "leaf")), check_vma=False,
    )
```

profile of v0, /device:TPU:10, one launch (start us, length us, event | category | flops | bytes accessed | tf_op | source)
XLA Modules:
  0.0 134.2 jit_solution(224621447760347970)
XLA Ops:
  0.0 0.1 and_select_fusion
  0.1 0.7 iota_compare_fusion
  0.8 0.1 iota_add_fusion
  0.9 0.1 add.41
  1.0 0.8 and_reduce_fusion
  1.7 0.1 copy.7
  1.8 0.1 broadcast_in_dim.24
  2.0 0.7 copy.8
  2.7 126.9 %shard_map.64 = f32[512,2048]{1,0:T(8,128)} custom-call(bf16[64,2048]{1,0:T(8,128)(2,1)} %points.1, bf16[512,2048]{1,0:T(8,128)(2,1)} %weights.1, bf16[512,2048]{1,0:T(8,128)(2,1)} %targets.1, f32[12,2048]{1,0:T(8,128)} %bitcast.8, s32[1,256]{1,0:T(1,128)} %skeleton.1), custom_call_target="tpu_custom_call" | custom-call | tf_op jit(solution)/shard_map/pallas_call | solution.py:357
  129.5 4.7 %copy.10 = f32[512,2048]{1,0:T(8,128)} copy(f32[512,2048]{1,0:T(8,128)} %shard_map.64) | data formatting | bytes 8388608
  (2 shorter events, 0.0 us)
where the time goes:
time: 134 us
  Pallas kernels  127 us (95%)
  local copies, waits for them, and re-layouts  5.68 us (4%)
  other arithmetic  1.66 us (1%)
    pallas_call x1, Pallas kernels, on_device(): pl.pallas_call(functools.partial(fused_kernel, n_clus, n_leaf), out_shape...  127 us
    unnamed x3, local copies, waits for them, and re-layouts  5.42 us

commit v1 on v0

--- a/solution.py
+++ b/solution.py
@@ -57,37 +57,41 @@
     return jnp.exp2(cross * (2.0 * scale) + (row_wide + (col_sq * -scale + bias)))
 
 
-def sweep_inverse(mats):
+def sweep_inverse(mats, beside):
     count, size = mats.shape[0], mats.shape[1]
-    row_id = lax.broadcasted_iota(jnp.int32, (count, size, 1), 1)
+    row_id = lax.broadcasted_iota(jnp.int32, (count, SWEEP, 1), 1)
     col_id = lax.broadcasted_iota(jnp.int32, (count, 1, size), 2)
 
-    def group(_, a):
+    def group(step, a):
+        beside(step)
+        panel = a[:, :SWEEP, :]
         for i in range(SWEEP):
-            row = a[:, i : i + 1, :]
-            col = a[:, :, i : i + 1]
-            inv = 1.0 / a[:, i : i + 1, i : i + 1]
+            row = panel[:, i : i + 1, :]
+            col = panel[:, :, i : i + 1]
+            inv = 1.0 / panel[:, i : i + 1, i : i + 1]
             row = jnp.where(col_id == i, -inv, row * inv)
             col = jnp.where(row_id == i, -1.0, col)
-            rest = jnp.where((row_id == i) | (col_id == i), 0.0, a)
-            a = rest - col * row
-        a = jnp.concatenate([a[:, SWEEP:, :], a[:, :SWEEP, :]], axis=1)
-        return pltpu.roll(a, size - SWEEP, 2)
+            panel = jnp.where((row_id == i) | (col_id == i), 0.0, panel) - col * row
+        below = a[:, SWEEP:, :]
+        rest = jnp.where(col_id < SWEEP, 0.0, below)
+        for i in range(SWEEP):
+            rest = rest - below[:, :, i : i + 1] * panel[:, i : i + 1, :]
+        return pltpu.roll(jnp.concatenate([rest, panel], axis=1), size - SWEEP, 2)
 
     return -lax.fori_loop(0, size // SWEEP, group, mats)
 
 
 def fused_kernel(
     n_clus, n_leaf,
-    points, weights, targets, bias, skeleton,
+    points, weights, targets, near_lists, tile_counts, skeleton,
     out,
-    window, win_p, win_sq, tiles, pick, prolong, gram, inv_high, inv_low, node_p, got_p,
+    bias, window, win_p, win_sq, tiles, pick, prolong, gram, inv_high, inv_low, node_p, got_p,
     node_r, got_r, sent_r, solved_buf,
     ps, pr, as_, ar, bs, br, qs, qr, ts, tr,
 ):
     clus, leaf = lax.axis_index("clus"), lax.axis_index("leaf")
     levels = n_leaf.bit_length() - 1
-    clusters = bias.shape[0] // 3
+    clusters, slots = near_lists.shape
     pts_cl = points.shape[1] // clusters
     n_skel = skeleton.shape[1]
     half = n_skel // 2
@@ -158,6 +162,20 @@
         def _():
             after.wait_recv()
 
+    spot = lax.broadcasted_iota(jnp.int32, (3 * clusters, 1), 0)
+    place_clus = jnp.where(
+        spot < clusters, clus,
+        jnp.where(spot < 2 * clusters, partner, jnp.where(even, clus - 1, clus + 1)),
+    )
+    spot_id = (place_clus * n_leaf + leaf) * clusters + lax.rem(spot, clusters)
+    spot_id = jnp.where((place_clus >= 0) & (place_clus < n_clus), spot_id, -1)
+    for k in range(clusters):
+        miss = jnp.full((3 * clusters, 1), -1e30, F32)
+        for s in range(slots):
+            hit = (spot_id == near_lists[k : k + 1, s : s + 1]) & (s < tile_counts[:, k : k + 1])
+            miss = jnp.where(hit, 0.0, miss)
+        bias[:, k * pts_cl : (k + 1) * pts_cl] = jnp.broadcast_to(miss, (3 * clusters, pts_cl))
+
     skel = skeleton[...]
     pick[...] = (
         lax.broadcasted_iota(jnp.int32, (points.shape[1], n_skel), 0) == skel
@@ -194,17 +212,53 @@
             base_p, own_sq_cols, points[:, cols], own_sq[:, cols]
         ).astype(BF16)
 
-    top_inv = sweep_inverse(gram[:, :half, :half])
+    def build(place, r):
+        rows = pl.ds(pl.multiple_of(r * 128, 128), 128)
+        q = pl.ds(place * clusters + r * 128 // pts_cl, 1)
+        for k in range(clusters):
+            cols = slice(k * pts_cl, (k + 1) * pts_cl)
+            tiles[place, rows, cols] = kernel_tile(
+                win_p[place, :, rows], win_sq[place, rows, :],
+                points[:, cols], own_sq[:, cols], bias[q, cols],
+            ).astype(BF16)
+
+    n_block = points.shape[1] // 128
+    n_step = half // SWEEP
+    per_step = -(-n_block // n_step)
+
+    def beside_top(step):
+        for t in range(per_step):
+            build(0, step * per_step + t)
+            build(1, step * per_step + t)
+
+    own_rows = weights.shape[0] * clusters // n_step
+
+    def beside_low(step):
+        for t in range(per_step):
+            build(2, step * per_step + t)
+        span = pl.ds(pl.multiple_of(step // clusters * own_rows, own_rows), own_rows)
+        cols = pl.ds(pl.multiple_of(lax.rem(step, clusters) * pts_cl, pts_cl), pts_cl)
+        out[span, cols] = (
+            targets[span, cols].astype(F32) - ridge_term * weights[span, cols].astype(F32)
+            - dot(weights[span, :], tiles[0, :, cols])
+        )
+
+    win_sq[0] = square_cols(win_p[0])
+    win_sq[1] = square_cols(win_p[1])
+    top_inv = sweep_inverse(gram[:, :half, :half], beside_top)
+    pass_on(first_w[0], next_w[0])
+    take(next_p)
+    win_sq[2] = square_cols(win_p[2])
     couple = [dot_full(top_inv[v], gram[v, :half, half:]) for v in range(levels + 1)]
     schur = jnp.stack([
         gram[v, half:, half:] - dot_full(gram[v, half:, :half], couple[v])
         for v in range(levels + 1)
     ])
-    pass_on(first_w[0], next_w[0])
     pass_on(first_w[1], next_w[1])
-    low_inv = sweep_inverse(schur)
     pass_on(first_w[2], next_w[2])
+    low_inv = sweep_inverse(schur, beside_low)
     pass_on(first_w[3], next_w[3])
+    pass_on(first_w[4], next_w[4])
     for v in range(levels + 1):
         cross = dot_full(couple[v], low_inv[v])
         corner = top_inv[v] + dot_full(cross, couple[v], ((1,), (1,)))
@@ -214,25 +268,18 @@
         ], axis=0)
         inv_high[v], inv_low[v] = split(whole)
 
-    take(next_p)
-    for place in range(3):
-        win_sq[...] = square_cols(win_p[place])
-
-        def build(r, _):
-            rows = pl.ds(pl.multiple_of(r * 128, 128), 128)
-            q = pl.ds(place * clusters + r * 128 // pts_cl, 1)
-            for k in range(clusters):
-                cols = slice(k * pts_cl, (k + 1) * pts_cl)
-                tiles[place, rows, cols] = kernel_tile(
-                    win_p[place, :, rows], win_sq[rows, :],
-                    points[:, cols], own_sq[:, cols], bias[q, cols],
-                ).astype(BF16)
-            return 0
-
-        lax.fori_loop(0, points.shape[1] // 128, build, 0)
-
     per = CHUNK // PIECE
-    passed = 4
+    passed = 5
+    for c in range(n_ch):
+        span = slice(c * CHUNK, (c + 1) * CHUNK)
+        while passed < n_piece and passed < max((c + 1) * per, 6 + c):
+            pass_on(first_w[passed], next_w[passed])
+            passed += 1
+
+        @pl.loop(0, clusters)
+        def _(k):
+            cols = pl.ds(pl.multiple_of(k * pts_cl, pts_cl), pts_cl)
+            out[span, cols] -= dot(window[0, span, :], tiles[1, :, cols])
 
     def exchange(c, level):
         at = c * levels + level
@@ -256,18 +303,6 @@
 
     def near_stage(c):
         span = slice(c * CHUNK, (c + 1) * CHUNK)
-        for i in range(max(passed, c * per), (c + 1) * per):
-            pass_on(first_w[i], next_w[i])
-        @pl.loop(0, clusters)
-        def _(k):
-            cols = pl.ds(pl.multiple_of(k * pts_cl, pts_cl), pts_cl)
-            near = dot(weights[span, :], tiles[0, :, cols]) + dot(
-                window[0, span, :], tiles[1, :, cols]
-            )
-            out[span, cols] = (
-                targets[span, cols].astype(F32) - ridge_term * weights[span, cols].astype(F32)
-                - near
-            )
         for i in range(c * per, (c + 1) * per):
             take(next_w[i])
         node_r[...] = jnp.zeros_like(node_r)
@@ -327,22 +362,6 @@
             next_w[i].wait_send()
 
 
-def near_bias(n_clus, n_leaf, pts_cl, near_lists, tile_counts):
-    clus, leaf = lax.axis_index("clus"), lax.axis_index("leaf")
-    clusters, slots = near_lists.shape
-    even = lax.rem(clus, 2) == 0
-    partner = jnp.where(even, clus + 1, clus - 1)
-    other = jnp.where(even, clus - 1, clus + 1)
-    place = jnp.stack([clus, partner, other])
-    valid = (place >= 0) & (place < n_clus)
-    first = jnp.where(valid, (place * n_leaf + leaf) * clusters, -clusters)
-    ident = (first[:, None] + jnp.arange(clusters)[None, :]).reshape(-1)
-    used = jnp.arange(slots)[None, :] < tile_counts[:, None]
-    hit = (near_lists[:, :, None] == ident[None, None, :]) & used[:, :, None]
-    bias = jnp.where(jnp.any(hit, axis=1), 0.0, -1e30).astype(F32)
-    return jnp.repeat(bias.T, pts_cl, axis=1)
-
-
 def on_device(n_clus, n_leaf, points, weights, targets, near_lists, tile_counts, skeleton):
     rhs, pts = weights.shape
     features = points.shape[0]
@@ -353,16 +372,16 @@
     n_piece, n_ch = rhs // PIECE, rhs // CHUNK
     vmem = pl.BlockSpec(memory_space=pltpu.VMEM)
     dma = pltpu.SemaphoreType.DMA
-    bias = near_bias(n_clus, n_leaf, pts // clusters, near_lists, tile_counts)
     return pl.pallas_call(
         functools.partial(fused_kernel, n_clus, n_leaf),
         out_shape=jax.ShapeDtypeStruct((rhs, pts), F32),
-        in_specs=[vmem] * 5,
+        in_specs=[vmem] * 6,
         out_specs=vmem,
         scratch_shapes=[
+            pltpu.VMEM((3 * clusters, pts), F32),
             pltpu.VMEM((2, rhs, pts), BF16),
             pltpu.VMEM((3, features, pts), BF16),
-            pltpu.VMEM((pts, 128), F32),
+            pltpu.VMEM((3, pts, 128), F32),
             pltpu.VMEM((3, pts, pts), BF16),
             pltpu.VMEM((pts, n_skel), BF16),
             pltpu.VMEM((n_skel, pts), BF16),
@@ -383,7 +402,7 @@
         compiler_params=pltpu.CompilerParams(
             collective_id=0, has_side_effects=True, vmem_limit_bytes=60 * 1024 * 1024
         ),
-    )(points, weights, targets, bias, skeleton)
+    )(points, weights, targets, near_lists, tile_counts.reshape(1, -1), skeleton)
 
 
 def solution(mesh):

time: 134 us -> 105 us (0.78)
  Pallas kernels: 127 us -> 100 us
  other arithmetic: 1.66 us -> 0 us
    pallas_call x1, Pallas kernels: 127 us -> 100 us  [on_device(): pl.pallas_call(functools.partial(fused_kernel, n_clus, n_leaf), out_shape...]
    unnamed x3 -> x1, local copies, waits for them, and re-layouts: 5.42 us -> 4.7 us
where the time goes in v1:
time: 105 us
  Pallas kernels  100 us (95%)
  local copies, waits for them, and re-layouts  4.7 us (4%)
    pallas_call x1, Pallas kernels, on_device(): pl.pallas_call(functools.partial(fused_kernel, n_clus, n_leaf), out_shape...  100 us
    unnamed x1, local copies, waits for them, and re-layouts  4.7 us

profile of v1, /device:TPU:10, one launch (start us, length us, event | category | flops | bytes accessed | tf_op | source)
XLA Modules:
  0.0 104.9 jit_solution(6013347660811526083)
XLA Ops:
  0.0 100.1 %shard_map.64 = f32[512,2048]{1,0:T(8,128)} custom-call(bf16[64,2048]{1,0:T(8,128)(2,1)} %points.1, bf16[512,2048]{1,0:T(8,128)(2,1)} %weights.1, bf16[512,2048]{1,0:T(8,128)(2,1)} %targets.1, s32[4,4]{1,0:T(4,128)} %near_lists.1, s32[1,4]{1,0:T(1,128)} %bitcast.1, s32[1,256]{1,0:T(1,128)} %skeleton.1), custom_call_target="tpu_custom_call" | custom-call | tf_op jit(solution)/shard_map/pallas_call | solution.py:375
  100.2 4.7 %copy.8 = f32[512,2048]{1,0:T(8,128)} copy(f32[512,2048]{1,0:T(8,128)} %shard_map.64) | data formatting | bytes 8388608

commit v2 on v1

--- a/solution.py
+++ b/solution.py
@@ -15,7 +15,7 @@
 SWEEP = 8
 LOG2E = 1.4426950408889634
 PIECE = 64
-CHUNK = 128
+CHUNK = 256
 
 
 def dot(a, b):
@@ -65,13 +65,21 @@
     def group(step, a):
         beside(step)
         panel = a[:, :SWEEP, :]
-        for i in range(SWEEP):
-            row = panel[:, i : i + 1, :]
-            col = panel[:, :, i : i + 1]
-            inv = 1.0 / panel[:, i : i + 1, i : i + 1]
-            row = jnp.where(col_id == i, -inv, row * inv)
-            col = jnp.where(row_id == i, -1.0, col)
-            panel = jnp.where((row_id == i) | (col_id == i), 0.0, panel) - col * row
+        for i in range(0, SWEEP, 2):
+            row0, row1 = panel[:, i : i + 1, :], panel[:, i + 1 : i + 2, :]
+            col0, col1 = panel[:, :, i : i + 1], panel[:, :, i + 1 : i + 2]
+            p00, p01, p11 = row0[:, :, i : i + 1], row0[:, :, i + 1 : i + 2], row1[:, :, i + 1 : i + 2]
+            inv = 1.0 / (p00 * p11 - p01 * p01)
+            i00, i01, i11 = p11 * inv, -p01 * inv, p00 * inv
+            new0 = i00 * row0 + i01 * row1
+            new1 = i01 * row0 + i11 * row1
+            new0 = jnp.where(col_id == i, -i00, jnp.where(col_id == i + 1, -i01, new0))
+            new1 = jnp.where(col_id == i, -i01, jnp.where(col_id == i + 1, -i11, new1))
+            row_in = (row_id == i) | (row_id == i + 1)
+            col_in = (col_id == i) | (col_id == i + 1)
+            col0 = jnp.where(row_in, jnp.where(row_id == i, -1.0, 0.0), col0)
+            col1 = jnp.where(row_in, jnp.where(row_id == i, 0.0, -1.0), col1)
+            panel = jnp.where(row_in | col_in, 0.0, panel) - col0 * new0 - col1 * new1
         below = a[:, SWEEP:, :]
         rest = jnp.where(col_id < SWEEP, 0.0, below)
         for i in range(SWEEP):
@@ -182,17 +190,30 @@
     ).astype(BF16)
     base_p = dot(points[...], pick[...]).astype(BF16)
     node_p[0] = base_p
+    own_sq_cols = square_cols(base_p)
+    own_sq = square_rows(points[...])
+
+    def build_prolong(k):
+        cols = slice(k * pts_cl, (k + 1) * pts_cl)
+        prolong[:, cols] = kernel_tile(
+            base_p, own_sq_cols, points[:, cols], own_sq[:, cols]
+        ).astype(BF16)
+
     for level, (upper, sibling) in enumerate(siblings):
         copy = remote(
             node_p.at[level, :, pl.ds(0, half)], got_p.at[level], qs.at[level], qr.at[level],
             (clus, sibling),
         )
         copy.start()
+        if level < clusters - 1:
+            build_prolong(level)
         copy.wait()
         mine, other = node_p[level, :, :half], got_p[level]
         node_p[level + 1, :, :half] = jnp.where(upper, other, mine)
         node_p[level + 1, :, half:] = jnp.where(upper, mine, other)
 
+    for k in range(min(levels, clusters - 1), clusters):
+        build_prolong(k)
     pass_on(first_p, next_p)
     win_p[0] = points[...]
     for level in range(levels + 1):
@@ -203,14 +224,6 @@
             node_shift, 0.0,
         )
         gram[level] = kernel_tile(p, square_cols(p), p, square_rows(p)) + shift_mat
-
-    own_sq_cols = square_cols(base_p)
-    own_sq = square_rows(points[...])
-    for k in range(clusters):
-        cols = slice(k * pts_cl, (k + 1) * pts_cl)
-        prolong[:, cols] = kernel_tile(
-            base_p, own_sq_cols, points[:, cols], own_sq[:, cols]
-        ).astype(BF16)
 
     def build(place, r):
         rows = pl.ds(pl.multiple_of(r * 128, 128), 128)

time: 105 us -> 124 us (1.18); the launches traced: 105 us -> 122 us
  Pallas kernels: 100 us -> 117 us
    pallas_call x1, Pallas kernels: 100 us -> 117 us  [on_device(): pl.pallas_call(functools.partial(fused_kernel, n_clus, n_leaf), out_shape...]
where the time goes in v2:
time: 124 us; the launch traced here: 122 us
  Pallas kernels  117 us (94%)
  local copies, waits for them, and re-layouts  4.7 us (4%)
    pallas_call x1, Pallas kernels, on_device(): pl.pallas_call(functools.partial(fused_kernel, n_clus, n_leaf), out_shape...  117 us
    unnamed x1, local copies, waits for them, and re-layouts  4.7 us

profile of v2, /device:TPU:10, one launch (start us, length us, event | category | flops | bytes accessed | tf_op | source)
XLA Modules:
  0.0 121.6 jit_solution(12537321237527558426)
XLA Ops:
  0.0 116.9 %shard_map.64 = f32[512,2048]{1,0:T(8,128)} custom-call(bf16[64,2048]{1,0:T(8,128)(2,1)} %points.1, bf16[512,2048]{1,0:T(8,128)(2,1)} %weights.1, bf16[512,2048]{1,0:T(8,128)(2,1)} %targets.1, s32[4,4]{1,0:T(4,128)} %near_lists.1, s32[1,4]{1,0:T(1,128)} %bitcast.1, s32[1,256]{1,0:T(1,128)} %skeleton.1), custom_call_target="tpu_custom_call" | custom-call | tf_op jit(solution)/shard_map/pallas_call | solution.py:388
  116.9 4.7 %copy.8 = f32[512,2048]{1,0:T(8,128)} copy(f32[512,2048]{1,0:T(8,128)} %shard_map.64) | data formatting | bytes 8388608

commit v3 on v2

--- a/solution.py
+++ b/solution.py
@@ -15,7 +15,7 @@
 SWEEP = 8
 LOG2E = 1.4426950408889634
 PIECE = 64
-CHUNK = 256
+CHUNK = 128
 
 
 def dot(a, b):

time: 124 us -> 117 us (0.944); the launches traced: 122 us -> 117 us
  Pallas kernels: 117 us -> 112 us
    pallas_call x1, Pallas kernels: 117 us -> 112 us  [on_device(): pl.pallas_call(functools.partial(fused_kernel, n_clus, n_leaf), out_shape...]
where the time goes in v3:
time: 117 us
  Pallas kernels  112 us (96%)
  local copies, waits for them, and re-layouts  4.7 us (4%)
    pallas_call x1, Pallas kernels, on_device(): pl.pallas_call(functools.partial(fused_kernel, n_clus, n_leaf), out_shape...  112 us
    unnamed x1, local copies, waits for them, and re-layouts  4.7 us

profile of v3, /device:TPU:10, one launch (start us, length us, event | category | flops | bytes accessed | tf_op | source)
XLA Modules:
  0.0 117.2 jit_solution(13773737767798776463)
XLA Ops:
  0.0 112.5 %shard_map.64 = f32[512,2048]{1,0:T(8,128)} custom-call(bf16[64,2048]{1,0:T(8,128)(2,1)} %points.1, bf16[512,2048]{1,0:T(8,128)(2,1)} %weights.1, bf16[512,2048]{1,0:T(8,128)(2,1)} %targets.1, s32[4,4]{1,0:T(4,128)} %near_lists.1, s32[1,4]{1,0:T(1,128)} %bitcast.1, s32[1,256]{1,0:T(1,128)} %skeleton.1), custom_call_target="tpu_custom_call" | custom-call | tf_op jit(solution)/shard_map/pallas_call | solution.py:388
  112.5 4.7 %copy.8 = f32[512,2048]{1,0:T(8,128)} copy(f32[512,2048]{1,0:T(8,128)} %shard_map.64) | data formatting | bytes 8388608
